TPU v7x, 32 devices: a whole 2x2x4 slice. The times are simulated.
32 devices in a mesh: dp: 8 (over z, x), mp: 4 (over y, core).
Axes of the slice: x: 2, y: 2, z: 4, core: 2. Of those that a mesh axis runs over, the one named last changes fastest.
Arguments:
- tokens: bfloat16 [49152, 1280], P(('dp', 'mp')), may hold values from -40 to 40, as said below
- lengths: int32 [768, 32], P('dp'), may hold values from 0 to 64, as said below
- cotangent: bfloat16 [49152, 1280], P(('dp', 'mp')), may hold values from -6 to 6
- query_weight: bfloat16 [1280, 1280], P(None, 'mp'), may hold values from -0.15625 to 0.15625
- key_weight: bfloat16 [1280, 1280], P(None, 'mp'), may hold values from -0.15625 to 0.15625
- value_weight: bfloat16 [1280, 1280], P(None, 'mp'), may hold values from -0.15625 to 0.15625
- out_weight: bfloat16 [1280, 1280], P('mp'), may hold values from -0.3125 to 0.3125
- up_weight: bfloat16 [1280, 5120], P(None, 'mp'), may hold values from -0.15625 to 0.15625
- hidden_bias: bfloat16 [5120], P('mp'), may hold values from -3 to 3
- down_weight: bfloat16 [5120, 1280], P('mp'), may hold values from -0.078125 to 0.078125
- output_bias: bfloat16 [1280], replicated, may hold values from -2 to 2
- first_gain: bfloat16 [1280], replicated, may hold values from 0.099609375 to 1.8984375
- second_gain: bfloat16 [1280], replicated, may hold values from 0.099609375 to 1.8984375
Outputs:
- layer_output: bfloat16 [49152, 1280], P(('dp', 'mp'))
- input_gradient: float32 [49152, 1280], P(('dp', 'mp'))
- query_gradient: float32 [1280, 1280], P(None, 'mp')
- key_gradient: float32 [1280, 1280], P(None, 'mp')
- value_gradient: float32 [1280, 1280], P(None, 'mp')
- out_gradient: float32 [1280, 1280], P('mp')
- up_gradient: float32 [1280, 5120], P(None, 'mp')
- hidden_bias_gradient: float32 [5120], P('mp')
- down_gradient: float32 [5120, 1280], P('mp')
- output_bias_gradient: float32 [1280], replicated
- first_gain_gradient: float32 [1280], replicated
- second_gain_gradient: float32 [1280], replicated
- rms_stats: float32 [3], replicated
Inputs may be any that keep to these rules, and one draw needn't show every extreme that they name: Each row lists the lengths of the series packed into it in order, zeros only after the last; every row holds one series or more and at most 64 patches; some row holds a single series of 64. `tokens`: activations of order one.
All inputs are finite; a program needn't handle non-finite values.
Results may differ from a plain program's by a relative error of at most 0.018.
Values may be sent and summed in bfloat16 or wider, within the bound.
A program may use at most 384 MiB of HBM per device.

v0:
```python
import math
import jax
import jax.numpy as jnp
from jax import lax
from jax.sharding import PartitionSpec as P

D = 1280
HD = 80
L = 64
SLOTS = 32
EPSILON = 1e-06
MASKED_SCORE = -1e30


def segments(lengths):
    ends = jnp.cumsum(lengths, axis=1)
    places = lax.broadcasted_iota(jnp.int32, (lengths.shape[0], L, lengths.shape[1]), 1)
    return jnp.sum((ends[:, None, :] <= places).astype(jnp.int32), axis=2)


def normalize(values, gain):
    scale_rows = lax.rsqrt(jnp.mean(values * values, axis=1, keepdims=True) + EPSILON)
    normed = (values * scale_rows * gain.astype(jnp.float32)).astype(jnp.bfloat16)
    return (scale_rows, normed)


def norm_back(values, scale_rows, gain, grad):
    weighted = gain.astype(jnp.float32) * grad
    inner = jnp.sum(weighted * values, axis=1, keepdims=True)
    gain_part = jnp.sum(grad * values * scale_rows, axis=0)
    back = (
        weighted * scale_rows
        - values * scale_rows * scale_rows * scale_rows * inner / values.shape[1]
    )
    return (gain_part, back)


def per_device(
    tokens,
    lengths,
    cotangent,
    query_weight,
    key_weight,
    value_weight,
    out_weight,
    up_weight,
    hidden_bias,
    down_weight,
    output_bias,
    first_gain,
    second_gain,
):
    local_rows = tokens.shape[0]
    width = query_weight.shape[1]
    heads_here = width // HD
    rows_here = lengths.shape[0]
    scale = 1.0 / math.sqrt(HD)
    segment_ids = segments(lengths)
    valid_all = (segment_ids < SLOTS).reshape(-1).astype(jnp.float32)
    valid = lax.dynamic_slice_in_dim(valid_all, lax.axis_index("mp") * local_rows, local_rows)
    causal = lax.broadcasted_iota(jnp.int32, (L, L), 1) <= lax.broadcasted_iota(
        jnp.int32, (L, L), 0
    )
    allowed = ((segment_ids[:, :, None] == segment_ids[:, None, :]) & causal[None])[:, None]
    inputs = tokens.astype(jnp.float32)
    first_scale, first_normed = normalize(inputs, first_gain)
    first_rows = lax.all_gather(first_normed, "mp", axis=0, tiled=True)
    joined_weight = jnp.concatenate([query_weight, key_weight, value_weight], axis=1)
    joined = jnp.dot(first_rows, joined_weight, preferred_element_type=jnp.float32).astype(
        jnp.bfloat16
    )
    queries = joined[:, :width].reshape(rows_here, L, heads_here, HD)
    keys = joined[:, width : 2 * width].reshape(rows_here, L, heads_here, HD)
    values = joined[:, 2 * width :].reshape(rows_here, L, heads_here, HD)

    def masked_scores():
        scores = (
            jnp.einsum("rqhe,rkhe->rhqk", queries, keys, preferred_element_type=jnp.float32) * scale
        )
        return jnp.where(allowed, scores, MASKED_SCORE)

    scores = masked_scores()
    peak = jnp.max(scores, axis=-1, keepdims=True)
    logsum = peak + jnp.log(jnp.sum(jnp.exp(scores - peak), axis=-1, keepdims=True))
    probs_low = jnp.exp(scores - logsum).astype(jnp.bfloat16)
    mixed = jnp.einsum("rhqk,rkhe->rqhe", probs_low, values, preferred_element_type=jnp.float32)
    mixed = mixed.astype(jnp.bfloat16).reshape(rows_here * L, width)
    attention_local = lax.psum_scatter(
        jnp.dot(mixed, out_weight, preferred_element_type=jnp.float32).astype(jnp.bfloat16),
        "mp",
        scatter_dimension=0,
        tiled=True,
    ).astype(jnp.float32)
    hidden = inputs + attention_local
    second_scale, second_normed = normalize(hidden, second_gain)
    second_rows = lax.all_gather(second_normed, "mp", axis=0, tiled=True)
    preact = jnp.dot(
        second_rows, up_weight, preferred_element_type=jnp.float32
    ) + hidden_bias.astype(jnp.float32)
    sigma = jax.nn.sigmoid(preact)
    active = (preact * sigma).astype(jnp.bfloat16)
    feed_local = lax.psum_scatter(
        jnp.dot(active, down_weight, preferred_element_type=jnp.float32).astype(jnp.bfloat16),
        "mp",
        scatter_dimension=0,
        tiled=True,
    ).astype(jnp.float32) + output_bias.astype(jnp.float32)
    result = hidden + feed_local
    mask_col = valid[:, None]
    squares = jnp.stack(
        [
            jnp.sum(mask_col * attention_local * attention_local),
            jnp.sum(mask_col * feed_local * feed_local),
            jnp.sum(mask_col * result * result),
        ]
    )
    count = jnp.sum(valid)
    grad_out = cotangent.astype(jnp.float32)
    output_bias_part = jnp.sum(grad_out, axis=0)
    grad_rows = lax.all_gather(cotangent, "mp", axis=0, tiled=True)
    down_part = jnp.einsum("tf,td->fd", active, grad_rows, preferred_element_type=jnp.float32)
    active_grad = jnp.einsum(
        "td,fd->tf", grad_rows, down_weight, preferred_element_type=jnp.float32
    )
    active_grad = active_grad.astype(jnp.bfloat16).astype(jnp.float32)
    preact_grad = (active_grad * (sigma + preact * sigma * (1.0 - sigma))).astype(jnp.bfloat16)
    bias_part = jnp.sum(preact_grad.astype(jnp.float32), axis=0)
    up_part = jnp.einsum("td,tf->df", second_rows, preact_grad, preferred_element_type=jnp.float32)
    second_grad = lax.psum_scatter(
        jnp.einsum("tf,df->td", preact_grad, up_weight, preferred_element_type=jnp.float32).astype(
            jnp.bfloat16
        ),
        "mp",
        scatter_dimension=0,
        tiled=True,
    ).astype(jnp.float32)
    second_gain_part, second_back = norm_back(hidden, second_scale, second_gain, second_grad)
    hidden_grad = grad_out + second_back
    branch_low = hidden_grad.astype(jnp.bfloat16)
    branch_grad = lax.all_gather(branch_low, "mp", axis=0, tiled=True)
    out_part = jnp.einsum("tk,td->kd", mixed, branch_grad, preferred_element_type=jnp.float32)
    mixed_grad = jnp.einsum(
        "td,kd->tk", branch_grad, out_weight, preferred_element_type=jnp.float32
    )
    mixed_grad = mixed_grad.astype(jnp.bfloat16).reshape(rows_here, L, heads_here, HD)
    probs = jnp.exp(masked_scores() - logsum)
    probs_grad = jnp.einsum(
        "rqhe,rkhe->rhqk", mixed_grad, values, preferred_element_type=jnp.float32
    )
    value_grad = jnp.einsum(
        "rhqk,rqhe->rkhe",
        probs.astype(jnp.bfloat16),
        mixed_grad,
        preferred_element_type=jnp.float32,
    ).astype(jnp.bfloat16)
    inner = jnp.sum(probs * probs_grad, axis=-1, keepdims=True)
    scores_grad = (probs * (probs_grad - inner)).astype(jnp.bfloat16)
    query_grad = (
        jnp.einsum("rhqk,rkhe->rqhe", scores_grad, keys, preferred_element_type=jnp.float32) * scale
    ).astype(jnp.bfloat16)
    key_grad = (
        jnp.einsum("rhqk,rqhe->rkhe", scores_grad, queries, preferred_element_type=jnp.float32)
        * scale
    ).astype(jnp.bfloat16)
    joined_grad = jnp.concatenate(
        [
            query_grad.reshape(rows_here * L, width),
            key_grad.reshape(rows_here * L, width),
            value_grad.reshape(rows_here * L, width),
        ],
        axis=1,
    )
    joined_part = jnp.einsum(
        "td,tk->dk", first_rows, joined_grad, preferred_element_type=jnp.float32
    )
    query_part = joined_part[:, :width]
    key_part = joined_part[:, width : 2 * width]
    value_part = joined_part[:, 2 * width :]
    first_grad = lax.psum_scatter(
        jnp.einsum(
            "tk,dk->td", joined_grad, joined_weight, preferred_element_type=jnp.float32
        ).astype(jnp.bfloat16),
        "mp",
        scatter_dimension=0,
        tiled=True,
    ).astype(jnp.float32)
    first_gain_part, first_back = norm_back(inputs, first_scale, first_gain, first_grad)
    input_gradient = hidden_grad + first_back
    query_total, key_total, value_total, out_total, up_total, bias_total, down_total = (
        lax.psum(query_part.astype(jnp.bfloat16), "dp").astype(jnp.float32),
        lax.psum(key_part.astype(jnp.bfloat16), "dp").astype(jnp.float32),
        lax.psum(value_part.astype(jnp.bfloat16), "dp").astype(jnp.float32),
        lax.psum(out_part.astype(jnp.bfloat16), "dp").astype(jnp.float32),
        lax.psum(up_part.astype(jnp.bfloat16), "dp").astype(jnp.float32),
        lax.psum(bias_part.astype(jnp.bfloat16), "dp").astype(jnp.float32),
        lax.psum(down_part.astype(jnp.bfloat16), "dp").astype(jnp.float32),
    )
    first_total, second_total, output_bias_total, squares_total, count_total = lax.psum(
        (first_gain_part, second_gain_part, output_bias_part, squares, count), ("dp", "mp")
    )
    rms_stats = jnp.sqrt(squares_total / (count_total * D))
    return (
        result.astype(jnp.bfloat16),
        input_gradient,
        query_total,
        key_total,
        value_total,
        out_total,
        up_total,
        bias_total,
        down_total,
        output_bias_total,
        first_total,
        second_total,
        rms_stats,
    )


def solution(mesh):
    return jax.shard_map(
        per_device,
        mesh=mesh,
        in_specs=(
            P(("dp", "mp"), None),
            P("dp", None),
            P(("dp", "mp"), None),
            P(None, "mp"),
            P(None, "mp"),
            P(None, "mp"),
            P("mp", None),
            P(None, "mp"),
            P("mp"),
            P("mp", None),
            P(),
            P(),
            P(),
        ),
        out_specs=(
            P(("dp", "mp"), None),
            P(("dp", "mp"), None),
            P(None, "mp"),
            P(None, "mp"),
            P(None, "mp"),
            P("mp", None),
            P(None, "mp"),
            P("mp"),
            P("mp", None),
            P(),
            P(),
            P(),
            P(),
        ),
        check_vma=False,
    )
```

profile of v0, /device:TPU:0, one launch (start us, length us, event | category | flops | bytes accessed | tf_op | source)
XLA Modules:
  0.0 1699.2 jit_solution(6496326896694240132)
XLA Ops:
  26.5 93.2 %all-gather.5.cloned.1.call-done = bf16[6144,1280]{1,0:T(8,128)(2,1)} async-done(((bf16[1536,1280]{1,0:T(8,128)(2,1)}), bf16[6144,1280]{1,0:T(8,128)(2,1)}) %all-gather.5.cloned.1.call-update) | async-done | bytes 15728656 | tf_op jit(solution)/shard_map/all_gather | solution.py:67
  119.6 19.1 %convolution_convert_fusion.5 = bf16[6144,960]{0,1:T(8,128)(2,1)S(1)} fusion(bf16[6144,1280]{1,0:T(8,128)(2,1)} %all-gather.5.cloned.1.call-done, bf16[1280,960]{0,1:T(8,128)(2,1)} %constant_dynamic-update-slice_fusion), kind=kOutput, calls=%fused_computation.25 | convolution fusion | flops 15105392640 | bytes 29982720 | tf_op jit(solution)/shard_map/dot_general | solution.py:69
  243.6 18.3 %copy.67 = bf16[96,64,4,80]{3,2,1,0:T(4,128)(2,1)} copy(bf16[96,64,4,80]{3,1,2,0:T(8,128)(2,1)} %convert_bitcast_fusion.1) | data formatting | bytes 7864320 | tf_op jit(solution)/shard_map/convert_element_type | solution.py:87
  286.9 119.3 %reduce-scatter.5.cloned.1.call-done = bf16[1536,1280]{1,0:T(8,128)(2,1)} async-done(((bf16[6144,1280]{1,0:T(8,128)(2,1)}), bf16[1536,1280]{1,0:T(8,128)(2,1)}) %reduce-scatter.5.cloned.1.call-update) | async-done | bytes 3932176 | tf_op jit(solution)/shard_map/reduce_scatter | solution.py:88
  415.6 99.5 %all-gather.7.cloned.1.call-done = bf16[6144,1280]{1,0:T(8,128)(2,1)} async-done(((bf16[1536,1280]{1,0:T(8,128)(2,1)}), bf16[6144,1280]{1,0:T(8,128)(2,1)}) %all-gather.7.cloned.1.call-update) | async-done | bytes 15728656 | tf_op jit(solution)/shard_map/all_gather | solution.py:96
  515.1 32.9 %fusion = (bf16[6144,1280]{1,0:T(8,128)(2,1)}, f32[6144,1280]{1,0:T(8,128)}) fusion(f32[1280]{0:T(1024)S(1)} %convert_element_type.161, bf16[6144,1280]{1,0:T(8,128)(2,1)} %all-gather.7.cloned.1.call-done, bf16[1280,1280]{1,0:T(8,128)(2,1)S(1)} %copy-done), kind=kOutput, calls=%fused_computation.3 | convolution fusion | flops 20179845120 | bytes 66196480 | tf_op jit(solution)/shard_map/dot_general | solution.py:97
  547.9 25.9 %convolution_convert_fusion.2 = bf16[6144,1280]{1,0:T(8,128)(2,1)} fusion(bf16[6144,1280]{1,0:T(8,128)(2,1)} %get-tuple-element.44, bf16[1280,1280]{1,0:T(8,128)(2,1)S(1)} %copy-done.38), kind=kOutput, calls=%fused_computation.6 | convolution fusion | flops 20140523520 | bytes 34734080 | tf_op jit(solution)/shard_map/dot_general | solution.py:103
  573.9 42.6 %all-gather.9.cloned.1.call-done = bf16[6144,1280]{1,0:T(8,128)(2,1)} async-done(((bf16[1536,1280]{1,0:T(8,128)(2,1)}), bf16[6144,1280]{1,0:T(8,128)(2,1)}) %all-gather.9.cloned.1.call-update) | async-done | bytes 15728656 | tf_op jit(solution)/shard_map/all_gather | solution.py:120
  616.5 38.5 %fusion.39 = (bf16[1280]{0:T(1024)(128)(2,1)}, bf16[6144,1280]{1,0:T(8,128)(2,1)}) fusion(f32[6144,1280]{1,0:T(8,128)} %get-tuple-element.45, f32[1280]{0:T(1024)S(1)} %convert_element_type.161, bf16[6144,1280]{1,0:T(8,128)(2,1)} %all-gather.9.cloned.1.call-done, bf16[1280,1280]{1,0:T(8,128)(2,1)} %param.22), kind=kOutput, calls=%fused_computation.89 | convolution fusion | flops 20234893312 | bytes 66199040 | tf_op jit(solution)/shard_map/td,fd->tf/dot_general | solution.py:122
  655.0 25.9 %convolution_convert_fusion = bf16[6144,1280]{1,0:T(8,128)(2,1)} fusion(bf16[6144,1280]{1,0:T(8,128)(2,1)} %get-tuple-element.49, bf16[1280,1280]{1,0:T(8,128)(2,1)S(1)} %copy-done), kind=kOutput, calls=%fused_computation.4 | convolution fusion | flops 20140523520 | bytes 34734080 | tf_op jit(solution)/shard_map/tf,df->td/dot_general | solution.py:130
  682.5 56.3 %reduce-scatter.7.cloned.1.call-done = bf16[1536,1280]{1,0:T(8,128)(2,1)} async-done(((bf16[6144,1280]{1,0:T(8,128)(2,1)}), bf16[1536,1280]{1,0:T(8,128)(2,1)}) %reduce-scatter.7.cloned.1.call-update) | async-done | bytes 3932176 | tf_op jit(solution)/shard_map/reduce_scatter | solution.py:102
  738.8 122.3 %reduce-scatter.9.cloned.1.call-done = bf16[1536,1280]{1,0:T(8,128)(2,1)} async-done(((bf16[6144,1280]{1,0:T(8,128)(2,1)}), bf16[1536,1280]{1,0:T(8,128)(2,1)}) %reduce-scatter.9.cloned.1.call-update) | async-done | bytes 3932176 | tf_op jit(solution)/shard_map/reduce_scatter | solution.py:129
  880.7 26.7 %convolution_convert_fusion.7 = bf16[1280,1280]{1,0:T(8,128)(2,1)} fusion(bf16[6144,1280]{1,0:T(8,128)(2,1)} %get-tuple-element.44, bf16[6144,1280]{1,0:T(8,128)(2,1)} %all-gather.9.cloned.1.call-done), kind=kOutput, calls=%fused_computation.59 | convolution fusion | flops 20134297600 | bytes 34734080 | tf_op jit(solution)/shard_map/tf,td->fd/dot_general | solution.py:121
  907.4 26.8 %convolution_convert_fusion.8 = bf16[1280,1280]{1,0:T(8,128)(2,1)} fusion(bf16[6144,1280]{1,0:T(8,128)(2,1)} %all-gather.7.cloned.1.call-done, bf16[6144,1280]{1,0:T(8,128)(2,1)} %get-tuple-element.49), kind=kOutput, calls=%fused_computation.60 | convolution fusion | flops 20134297600 | bytes 34734080 | tf_op jit(solution)/shard_map/td,tf->df/dot_general | solution.py:128
  934.1 46.6 %all-gather.11.cloned.1.call-done = bf16[6144,1280]{1,0:T(8,128)(2,1)} async-done(((bf16[1536,1280]{1,0:T(8,128)(2,1)}), bf16[6144,1280]{1,0:T(8,128)(2,1)}) %all-gather.11.cloned.1.call-update) | async-done | bytes 15728656 | tf_op jit(solution)/shard_map/all_gather | solution.py:140
  1076.2 18.3 %copy.77 = bf16[96,64,4,80]{3,2,1,0:T(4,128)(2,1)} copy(bf16[96,64,4,80]{3,1,2,0:T(8,128)(2,1)} %convert_bitcast_fusion) | data formatting | bytes 7864320 | tf_op jit(solution)/shard_map/convert_element_type | solution.py:155
  1105.2 18.5 %copy.73 = bf16[96,64,4,80]{3,2,1,0:T(4,128)(2,1)} copy(bf16[96,64,4,80]{3,1,2,0:T(8,128)(2,1)} %fusion.26) | data formatting | bytes 7864320 | tf_op jit(solution)/shard_map/convert_element_type | solution.py:160
  1134.6 18.3 %copy.75 = bf16[96,64,4,80]{3,2,1,0:T(4,128)(2,1)} copy(bf16[96,64,4,80]{3,1,2,0:T(8,128)(2,1)} %fusion.27) | data formatting | bytes 7864320 | tf_op jit(solution)/shard_map/convert_element_type | solution.py:164
  1163.6 20.7 %fusion.30 = bf16[1280,960]{0,1:T(8,128)(2,1)S(1)} fusion(bf16[6144,1280]{1,0:T(8,128)(2,1)} %all-gather.5.cloned.1.call-done, bf16[6144,320]{1,0:T(8,128)(2,1)} %reshape.110, bf16[6144,320]{1,0:T(8,128)(2,1)} %reshape.109, bf16[6144,320]{1,0:T(8,128)(2,1)} %reshape.108), kind=kOutput, calls=%fused_computation.68 | convolution fusion | flops 15136112640 | bytes 29982720 | tf_op jit(solution)/shard_map/td,tk->dk/dot_general | solution.py:173
  1199.0 23.2 %convolution_convert_fusion.4 = bf16[6144,1280]{1,0:T(8,128)(2,1)} fusion(bf16[1280,960]{0,1:T(8,128)(2,1)} %constant_dynamic-update-slice_fusion, bf16[6144,320]{1,0:T(8,128)(2,1)} %reshape.110, bf16[6144,320]{1,0:T(8,128)(2,1)} %reshape.109, bf16[6144,320]{1,0:T(8,128)(2,1)} %reshape.108), kind=kOutput, calls=%fused_computation.8 | convolution fusion | flops 15142748160 | bytes 29982720 | tf_op jit(solution)/shard_map/tk,dk->td/dot_general | solution.py:180
  1222.8 22.8 %psum.89 = bf16[1280]{0:T(1024)(128)(2,1)S(1)} all-reduce(bf16[1280]{0:T(1024)(128)(2,1)S(1)} %copy-done.37), channel_id=1, replica_groups=mesh['dp'=8,'mp'=4] {'dp'}, use_global_device_ids=true, to_apply=%region_19.20 | all-reduce | flops 1280 | bytes 5120 | tf_op jit(solution)/shard_map/psum | solution.py:195
  1248.3 263.4 %all-reduce.4.cloned.1.call-done = (bf16[1280,320]{0,1:T(8,128)(2,1)}, bf16[1280,320]{0,1:T(8,128)(2,1)}, bf16[1280,320]{0,1:T(8,128)(2,1)}, bf16[320,1280]{1,0:...) async-done(((bf16[1280,320]{0,1:T(8,128)(2,1)}, bf16[1280,320]{0,1:T(8,128)(2,1)}, bf16[1280,320]{0,1:T(8,128)(2,1)}, bf16[320,1280]{1,0:T(8,128)(2,1)}, ...) | async-done | bytes 9830416 | tf_op jit(solution)/shard_map/psum | solution.py:190
  1529.6 103.7 %reduce-scatter.11.cloned.1.call-done = bf16[1536,1280]{1,0:T(8,128)(2,1)} async-done(((bf16[6144,1280]{1,0:T(8,128)(2,1)}), bf16[1536,1280]{1,0:T(8,128)(2,1)}) %reduce-scatter.11.cloned.1.call-update) | async-done | bytes 3932176 | tf_op jit(solution)/shard_map/reduce_scatter | solution.py:179
  1651.3 40.0 %all-reduce = (f32[1280]{0:T(1024)}, f32[1280]{0:T(1024)}, f32[1280]{0:T(1024)}, f32[3]{0:T(128)S(1)}, f32[]{:T(128)}) all-reduce(f32[1280]{0:T(1024)S(1)} %get-tuple-element.37, f32[1280]{0:T(1024)S(1)} %get-tuple-element.16, f32[1280]{0:T(1024)S(1)} %copy-done.32, ...), channel_id=1, replica_groups=mesh['dp'=8,'mp'=4] {'dp','mp'}, use_global_device_ids=true, to_apply=%region_22.23 | all-reduce | flops 3844 | bytes 30752 | tf_op jit(solution)/shard_map/psum | solution.py:198
  (166 shorter events, 361.5 us)
Async XLA Ops:
  7.2 507.9 %copy-start = (bf16[1280,1280]{1,0:T(8,128)(2,1)S(1)}, bf16[1280,1280]{1,0:T(8,128)(2,1)}, u32[]{:S(2)}) copy-start(bf16[1280,1280]{1,0:T(8,128)(2,1)} %param.20) | copy-start | bytes 9830404
  7.2 112.4 %all-gather.5.cloned.1.call-start = ((), (), s32[]{:S(2)}) async-start(), calls=%async_computation.4 | async-start | bytes 19660800 | tf_op jit(solution)/shard_map/all_gather | solution.py:67
  16.8 389.4 %reduce-scatter.5.cloned.1.call-start = ((), (), s32[]{:S(2)}) async-start(), calls=%async_computation.5 | async-start | bytes 19660800 | tf_op jit(solution)/shard_map/reduce_scatter | solution.py:88
  17.4 121.3 %copy-start.18 = (s32[96,64]{0,1:T(8,128)}, s32[96,64]{0,1:T(8,128)S(1)}, u32[]{:S(2)}) copy-start(s32[96,64]{0,1:T(8,128)S(1)} %convert_reduce_fusion.1) | copy-start | bytes 73732
  286.2 228.8 %all-gather.7.cloned.1.call-start = ((), (), s32[]{:S(2)}) async-start(), calls=%async_computation.6 | async-start | bytes 19660800 | tf_op jit(solution)/shard_map/all_gather | solution.py:96
  286.9 128.0 %copy-start.20 = (f32[1280]{0:T(1024)}, f32[1280]{0:T(1024)S(1)}, u32[]{:S(2)}) copy-start(f32[1280]{0:T(1024)S(1)} %convert_element_type.159) | copy-start | bytes 15364
  415.0 201.5 %all-gather.9.cloned.1.call-start = ((), (), s32[]{:S(2)}) async-start(), calls=%async_computation.8 | async-start | bytes 19660800 | tf_op jit(solution)/shard_map/all_gather | solution.py:120
  415.5 323.3 %reduce-scatter.7.cloned.1.call-start = ((), (), s32[]{:S(2)}) async-start(), calls=%async_computation.7 | async-start | bytes 19660800 | tf_op jit(solution)/shard_map/reduce_scatter | solution.py:102
  515.1 32.9 %copy-start.38 = (bf16[1280,1280]{1,0:T(8,128)(2,1)S(1)}, bf16[1280,1280]{1,0:T(8,128)(2,1)}, u32[]{:S(2)}) copy-start(bf16[1280,1280]{1,0:T(8,128)(2,1)} %param.22) | copy-start | bytes 9830404
  573.9 287.3 %reduce-scatter.9.cloned.1.call-start = ((), (), s32[]{:S(2)}) async-start(), calls=%async_computation.9 | async-start | bytes 19660800 | tf_op jit(solution)/shard_map/reduce_scatter | solution.py:129
  680.9 180.3 %copy-start.21 = (f32[1280]{0:T(1024)S(1)}, f32[1280]{0:T(1024)}, u32[]{:S(2)}) copy-start(f32[1280]{0:T(1024)} %copy-done.20) | copy-start | bytes 15364
  680.9 180.3 %copy-start.24 = (f32[1536]{0:T(1024)S(1)}, f32[1536]{0:T(1024)}, u32[]{:S(2)}) copy-start(f32[1536]{0:T(1024)} %copy-done.23) | copy-start | bytes 18436
  680.9 299.8 %all-gather.11.cloned.1.call-start = ((), (), s32[]{:S(2)}) async-start(), calls=%async_computation.10 | async-start | bytes 19660800 | tf_op jit(solution)/shard_map/all_gather | solution.py:140
  861.2 14.1 copy-start.3
  861.2 14.1 copy-start.6
  880.6 631.1 %all-reduce.4.cloned.1.call-start = ((), (), s32[]{:S(2)}) async-start(), calls=%async_computation.12 | async-start | bytes 19660800 | tf_op jit(solution)/shard_map/psum | solution.py:190
  907.4 73.4 %copy-start.39 = (bf16[320,1280]{1,0:T(8,128)(2,1)S(1)}, bf16[320,1280]{1,0:T(8,128)(2,1)}, u32[]{:S(2)}) copy-start(bf16[320,1280]{1,0:T(8,128)(2,1)} %param.19) | copy-start | bytes 2457604
  1198.9 434.4 %reduce-scatter.11.cloned.1.call-start = ((), (), s32[]{:S(2)}) async-start(), calls=%async_computation.11 | async-start | bytes 19660800 | tf_op jit(solution)/shard_map/reduce_scatter | solution.py:179
  1520.5 112.8 %copy-start.27 = (f32[1280]{0:T(1024)S(1)}, f32[1280]{0:T(1024)}, u32[]{:S(2)}) copy-start(f32[1280]{0:T(1024)} %copy-done.26) | copy-start | bytes 15364
  1520.5 112.8 %copy-start.29 = (f32[1536]{0:T(1024)S(1)}, f32[1536]{0:T(1024)}, u32[]{:S(2)}) copy-start(f32[1536]{0:T(1024)} %copy-done.28) | copy-start | bytes 18436
  1525.1 113.8 %copy-start.22 = (f32[1280]{0:T(1024)S(1)}, f32[1280]{0:T(1024)}, u32[]{:S(2)}) copy-start(f32[1280]{0:T(1024)} %copy-done.20) | copy-start | bytes 15364
  1525.1 113.8 %copy-start.25 = (f32[1536]{0:T(1024)S(1)}, f32[1536]{0:T(1024)}, u32[]{:S(2)}) copy-start(f32[1536]{0:T(1024)} %copy-done.23) | copy-start | bytes 18436
  1525.1 113.8 %copy-start.31 = (f32[1536]{0:T(1024)S(1)}, f32[1536]{0:T(1024)}, u32[]{:S(2)}) copy-start(f32[1536]{0:T(1024)} %copy-done.30) | copy-start | bytes 18436
  1638.9 53.6 %copy-start.1 = (bf16[1280,1280]{1,0:T(8,128)(2,1)S(1)}, bf16[1280,1280]{1,0:T(8,128)(2,1)}, u32[]{:S(2)}) copy-start(bf16[1280,1280]{1,0:T(8,128)(2,1)} %param.20) | copy-start | bytes 9830404
  (27 other events, 173.8 us)
Sparse Core Ops, SparseCore 0:
  16.9 102.6 all-gather.4
  286.4 119.8 reduce-scatter.4
  415.1 99.9 all-gather.6
  516.5 99.9 all-gather.8
  618.9 119.8 reduce-scatter.6
  741.3 119.8 reduce-scatter.8
  880.7 99.9 all-gather.10
  1199.0 312.5 all-reduce.3
  1514.5 118.8 reduce-scatter.10
where the time goes:
time: 1710 us; the launch traced here: 1700 us
  waiting for transfers between devices  948 us (55%)
  matrix products  346 us (20%)
  local copies, waits for them, and re-layouts  229 us (13%)
  other arithmetic  98.5 us (6%)
  blocking collectives  62.8 us (4%)
    psum x1, waiting for transfers between devices, per_device(): lax.psum(query_part.astype(jnp.bfloat16), 'dp').astype(jnp.float32)  263 us
    reduce_scatter x1, waiting for transfers between devices, per_device(): lax.psum_scatter(jnp.einsum('tf,df->td', preact_grad, up_weight, preferre...  122 us
    reduce_scatter x1, waiting for transfers between devices, per_device(): lax.psum_scatter(jnp.dot(mixed, out_weight, preferred_element_type=jnp.fl...  119 us
    reduce_scatter x1, waiting for transfers between devices, per_device(): lax.psum_scatter(jnp.einsum('tk,dk->td', joined_grad, joined_weight, pref...  104 us
    all_gather x1, waiting for transfers between devices, per_device(): second_rows = lax.all_gather(second_normed, 'mp', axis=0, tiled=True)  99.5 us
    all_gather x1, waiting for transfers between devices, per_device(): first_rows = lax.all_gather(first_normed, 'mp', axis=0, tiled=True)  93.2 us
    reduce_scatter x1, waiting for transfers between devices, per_device(): lax.psum_scatter(jnp.dot(active, down_weight, preferred_element_type=jnp....  56.3 us
    all_gather x1, waiting for transfers between devices, per_device(): branch_grad = lax.all_gather(branch_low, 'mp', axis=0, tiled=True)  46.6 us
  transfers between devices with their start and end apart: 9, of which 9 were waited for; matrix products, arithmetic and copies ran while one was open for 14% of the time, Pallas kernels for 0%

commit v1 on v0

--- a/solution.py
+++ b/solution.py
@@ -10,6 +10,19 @@
 SLOTS = 32
 EPSILON = 1e-06
 MASKED_SCORE = -1e30
+
+
+def ring_gather(array, axis, dim):
+    ways = lax.axis_size(axis)
+    up = [(d, (d + 1) % ways) for d in range(ways)]
+    down = [(d, (d - 1) % ways) for d in range(ways)]
+    earlier, later = ([array], [array])
+    for _ in range(ways // 2):
+        earlier.append(lax.ppermute(earlier[-1], axis, up))
+    for _ in range((ways - 1) // 2):
+        later.append(lax.ppermute(later[-1], axis, down))
+    line = jnp.concatenate([*earlier[::-1], *later[1:]], axis=dim)
+    return jnp.roll(line, (lax.axis_index(axis) - ways // 2) * array.shape[dim], axis=dim)
 
 
 def segments(lengths):
@@ -137,7 +150,7 @@
     second_gain_part, second_back = norm_back(hidden, second_scale, second_gain, second_grad)
     hidden_grad = grad_out + second_back
     branch_low = hidden_grad.astype(jnp.bfloat16)
-    branch_grad = lax.all_gather(branch_low, "mp", axis=0, tiled=True)
+    branch_grad = ring_gather(branch_low, "mp", 0)
     out_part = jnp.einsum("tk,td->kd", mixed, branch_grad, preferred_element_type=jnp.float32)
     mixed_grad = jnp.einsum(
         "td,kd->tk", branch_grad, out_weight, preferred_element_type=jnp.float32

time: 1710 us -> 1750 us (1.023)
  local copies, waits for them, and re-layouts: 229 us -> 255 us
  waiting for transfers between devices: 948 us -> 968 us
    ppermute x0 -> x3, waiting for transfers between devices: none -> 64.9 us  [the longest x2 50.3 us: ring_gather(): earlier.append(lax.ppermute(earlier[-1], axis, up))]
    all_gather x1 -> x0, waiting for transfers between devices: 46.6 us -> none  [per_device(): branch_grad = lax.all_gather(branch_low, 'mp', axis=0, tiled=True)]
    unnamed x87 -> x98, local copies, waits for them, and re-layouts: 10.5 us -> 34.3 us
  transfers between devices with their start and end apart: 9 -> 11, of which waited for: 9 -> 11; matrix products, arithmetic and copies ran while one was open for 14% -> 14% of each run, Pallas kernels for 0% -> 0%
where the time goes in v1:
time: 1750 us; the launch traced here: 1740 us
  waiting for transfers between devices  968 us (55%)
  matrix products  343 us (20%)
  local copies, waits for them, and re-layouts  255 us (15%)
  other arithmetic  98.1 us (6%)
  blocking collectives  63 us (4%)
    psum x1, waiting for transfers between devices, per_device(): lax.psum(query_part.astype(jnp.bfloat16), 'dp').astype(jnp.float32)  265 us
    reduce_scatter x1, waiting for transfers between devices, per_device(): lax.psum_scatter(jnp.einsum('tf,df->td', preact_grad, up_weight, preferre...  122 us
    reduce_scatter x1, waiting for transfers between devices, per_device(): lax.psum_scatter(jnp.dot(mixed, out_weight, preferred_element_type=jnp.fl...  119 us
    reduce_scatter x1, waiting for transfers between devices, per_device(): lax.psum_scatter(jnp.einsum('tk,dk->td', joined_grad, joined_weight, pref...  104 us
    all_gather x1, waiting for transfers between devices, per_device(): second_rows = lax.all_gather(second_normed, 'mp', axis=0, tiled=True)  99.5 us
    all_gather x1, waiting for transfers between devices, per_device(): first_rows = lax.all_gather(first_normed, 'mp', axis=0, tiled=True)  93.4 us
    reduce_scatter x1, waiting for transfers between devices, per_device(): lax.psum_scatter(jnp.dot(active, down_weight, preferred_element_type=jnp....  56.3 us
    ppermute x2, waiting for transfers between devices, ring_gather(): earlier.append(lax.ppermute(earlier[-1], axis, up))  50.3 us
  transfers between devices with their start and end apart: 11, of which 11 were waited for; matrix products, arithmetic and copies ran while one was open for 14% of the time, Pallas kernels for 0%

profile of v1, /device:TPU:0, one launch (start us, length us, event | category | flops | bytes accessed | tf_op | source)
XLA Modules:
  0.0 1744.8 jit_solution(16346501392932742059)
XLA Ops:
  26.2 93.4 %all-gather.4.cloned.1.call-done = bf16[6144,1280]{1,0:T(8,128)(2,1)} async-done(((bf16[1536,1280]{1,0:T(8,128)(2,1)}), bf16[6144,1280]{1,0:T(8,128)(2,1)}) %all-gather.4.cloned.1.call-update) | async-done | bytes 15728656 | tf_op jit(solution)/shard_map/all_gather | solution.py:80
  119.7 19.1 %convolution_convert_fusion.5 = bf16[6144,960]{0,1:T(8,128)(2,1)S(1)} fusion(bf16[6144,1280]{1,0:T(8,128)(2,1)} %all-gather.4.cloned.1.call-done, bf16[1280,960]{0,1:T(8,128)(2,1)} %constant_dynamic-update-slice_fusion), kind=kOutput, calls=%fused_computation.29 | convolution fusion | flops 15105392640 | bytes 29982720 | tf_op jit(solution)/shard_map/dot_general | solution.py:82
  243.7 18.5 %copy.67 = bf16[96,64,4,80]{3,2,1,0:T(4,128)(2,1)} copy(bf16[96,64,4,80]{3,1,2,0:T(8,128)(2,1)} %convert_bitcast_fusion.1) | data formatting | bytes 7864320 | tf_op jit(solution)/shard_map/convert_element_type | solution.py:100
  287.2 119.3 %reduce-scatter.5.cloned.1.call-done = bf16[1536,1280]{1,0:T(8,128)(2,1)} async-done(((bf16[6144,1280]{1,0:T(8,128)(2,1)}), bf16[1536,1280]{1,0:T(8,128)(2,1)}) %reduce-scatter.5.cloned.1.call-update) | async-done | bytes 3932176 | tf_op jit(solution)/shard_map/reduce_scatter | solution.py:101
  415.9 99.5 %all-gather.6.cloned.1.call-done = bf16[6144,1280]{1,0:T(8,128)(2,1)} async-done(((bf16[1536,1280]{1,0:T(8,128)(2,1)}), bf16[6144,1280]{1,0:T(8,128)(2,1)}) %all-gather.6.cloned.1.call-update) | async-done | bytes 15728656 | tf_op jit(solution)/shard_map/all_gather | solution.py:109
  515.4 32.7 %fusion = (bf16[6144,1280]{1,0:T(8,128)(2,1)}, f32[6144,1280]{1,0:T(8,128)}) fusion(f32[1280]{0:T(1024)S(1)} %convert_element_type.161, bf16[6144,1280]{1,0:T(8,128)(2,1)} %all-gather.6.cloned.1.call-done, bf16[1280,1280]{1,0:T(8,128)(2,1)S(1)} %copy-done), kind=kOutput, calls=%fused_computation.3 | convolution fusion | flops 20179845120 | bytes 66196480 | tf_op jit(solution)/shard_map/dot_general | solution.py:110
  548.1 25.9 %convolution_convert_fusion.2 = bf16[6144,1280]{1,0:T(8,128)(2,1)} fusion(bf16[6144,1280]{1,0:T(8,128)(2,1)} %get-tuple-element.44, bf16[1280,1280]{1,0:T(8,128)(2,1)S(1)} %copy-done.38), kind=kOutput, calls=%fused_computation.6 | convolution fusion | flops 20140523520 | bytes 34734080 | tf_op jit(solution)/shard_map/dot_general | solution.py:116
  574.1 42.7 %all-gather.8.cloned.1.call-done = bf16[6144,1280]{1,0:T(8,128)(2,1)} async-done(((bf16[1536,1280]{1,0:T(8,128)(2,1)}), bf16[6144,1280]{1,0:T(8,128)(2,1)}) %all-gather.8.cloned.1.call-update) | async-done | bytes 15728656 | tf_op jit(solution)/shard_map/all_gather | solution.py:133
  616.8 38.5 %fusion.51 = (bf16[1280]{0:T(1024)(128)(2,1)}, bf16[6144,1280]{1,0:T(8,128)(2,1)}) fusion(f32[6144,1280]{1,0:T(8,128)} %get-tuple-element.45, f32[1280]{0:T(1024)S(1)} %convert_element_type.161, bf16[6144,1280]{1,0:T(8,128)(2,1)} %all-gather.8.cloned.1.call-done, bf16[1280,1280]{1,0:T(8,128)(2,1)} %param.22), kind=kOutput, calls=%fused_computation.103 | convolution fusion | flops 20234893312 | bytes 66199040 | tf_op jit(solution)/shard_map/td,fd->tf/dot_general | solution.py:135
  655.3 25.9 %convolution_convert_fusion = bf16[6144,1280]{1,0:T(8,128)(2,1)} fusion(bf16[6144,1280]{1,0:T(8,128)(2,1)} %get-tuple-element.49, bf16[1280,1280]{1,0:T(8,128)(2,1)S(1)} %copy-done), kind=kOutput, calls=%fused_computation.4 | convolution fusion | flops 20140523520 | bytes 34734080 | tf_op jit(solution)/shard_map/tf,df->td/dot_general | solution.py:143
  682.8 56.3 %reduce-scatter.7.cloned.1.call-done = bf16[1536,1280]{1,0:T(8,128)(2,1)} async-done(((bf16[6144,1280]{1,0:T(8,128)(2,1)}), bf16[1536,1280]{1,0:T(8,128)(2,1)}) %reduce-scatter.7.cloned.1.call-update) | async-done | bytes 3932176 | tf_op jit(solution)/shard_map/reduce_scatter | solution.py:115
  739.2 122.3 %reduce-scatter.9.cloned.1.call-done = bf16[1536,1280]{1,0:T(8,128)(2,1)} async-done(((bf16[6144,1280]{1,0:T(8,128)(2,1)}), bf16[1536,1280]{1,0:T(8,128)(2,1)}) %reduce-scatter.9.cloned.1.call-update) | async-done | bytes 3932176 | tf_op jit(solution)/shard_map/reduce_scatter | solution.py:142
  880.9 45.4 %collective-permute-done = bf16[1536,1280]{1,0:T(8,128)(2,1)} collective-permute-done((bf16[1536,1280]{1,0:T(8,128)(2,1)}, bf16[1536,1280]{1,0:T(8,128)(2,1)}, u32[]{:S(2)}, u32[]{:S(2)}) %collective-permute-start) | collective-permute-done | bytes 3932192 | tf_op jit(solution)/shard_map/ppermute | solution.py:21
  926.3 26.7 %convolution_convert_fusion.6 = bf16[1280,1280]{1,0:T(8,128)(2,1)} fusion(bf16[6144,1280]{1,0:T(8,128)(2,1)} %get-tuple-element.44, bf16[6144,1280]{1,0:T(8,128)(2,1)} %all-gather.8.cloned.1.call-done), kind=kOutput, calls=%fused_computation.63 | convolution fusion | flops 20134297600 | bytes 34734080 | tf_op jit(solution)/shard_map/tf,td->fd/dot_general | solution.py:134
  954.7 26.8 %convolution_convert_fusion.7 = bf16[1280,1280]{1,0:T(8,128)(2,1)} fusion(bf16[6144,1280]{1,0:T(8,128)(2,1)} %all-gather.6.cloned.1.call-done, bf16[6144,1280]{1,0:T(8,128)(2,1)} %get-tuple-element.49), kind=kOutput, calls=%fused_computation.64 | convolution fusion | flops 20134297600 | bytes 34734080 | tf_op jit(solution)/shard_map/td,tf->df/dot_general | solution.py:141
  1132.9 18.3 %copy.77 = bf16[96,64,4,80]{3,2,1,0:T(4,128)(2,1)} copy(bf16[96,64,4,80]{3,1,2,0:T(8,128)(2,1)} %convert_bitcast_fusion) | data formatting | bytes 7864320 | tf_op jit(solution)/shard_map/convert_element_type | solution.py:168
  1162.0 18.5 %copy.73 = bf16[96,64,4,80]{3,2,1,0:T(4,128)(2,1)} copy(bf16[96,64,4,80]{3,1,2,0:T(8,128)(2,1)} %fusion.33) | data formatting | bytes 7864320 | tf_op jit(solution)/shard_map/convert_element_type | solution.py:173
  1191.3 18.3 %copy.75 = bf16[96,64,4,80]{3,2,1,0:T(4,128)(2,1)} copy(bf16[96,64,4,80]{3,1,2,0:T(8,128)(2,1)} %fusion.34) | data formatting | bytes 7864320 | tf_op jit(solution)/shard_map/convert_element_type | solution.py:177
  1220.4 20.7 %fusion.37 = bf16[1280,960]{0,1:T(8,128)(2,1)S(1)} fusion(bf16[6144,1280]{1,0:T(8,128)(2,1)} %all-gather.4.cloned.1.call-done, bf16[6144,320]{1,0:T(8,128)(2,1)} %reshape.110, bf16[6144,320]{1,0:T(8,128)(2,1)} %reshape.109, bf16[6144,320]{1,0:T(8,128)(2,1)} %reshape.108), kind=kOutput, calls=%fused_computation.72 | convolution fusion | flops 15136112640 | bytes 29982720 | tf_op jit(solution)/shard_map/td,tk->dk/dot_general | solution.py:186
  1242.6 22.9 %convolution_convert_fusion.4 = bf16[6144,1280]{1,0:T(8,128)(2,1)} fusion(bf16[1280,960]{0,1:T(8,128)(2,1)} %constant_dynamic-update-slice_fusion, bf16[6144,320]{1,0:T(8,128)(2,1)} %reshape.110, bf16[6144,320]{1,0:T(8,128)(2,1)} %reshape.109, bf16[6144,320]{1,0:T(8,128)(2,1)} %reshape.108), kind=kOutput, calls=%fused_computation.8 | convolution fusion | flops 15142748160 | bytes 29982720 | tf_op jit(solution)/shard_map/tk,dk->td/dot_general | solution.py:193
  1266.3 23.0 %psum.89 = bf16[1280]{0:T(1024)(128)(2,1)S(1)} all-reduce(bf16[1280]{0:T(1024)(128)(2,1)S(1)} %copy-done.37), channel_id=1, replica_groups=mesh['dp'=8,'mp'=4] {'dp'}, use_global_device_ids=true, to_apply=%region_19.20 | all-reduce | flops 1280 | bytes 5120 | tf_op jit(solution)/shard_map/psum | solution.py:208
  1291.8 265.1 %all-reduce.4.cloned.1.call-done = (bf16[1280,320]{0,1:T(8,128)(2,1)}, bf16[1280,320]{0,1:T(8,128)(2,1)}, bf16[1280,320]{0,1:T(8,128)(2,1)}, bf16[320,1280]{1,0:...) async-done(((bf16[1280,320]{0,1:T(8,128)(2,1)}, bf16[1280,320]{0,1:T(8,128)(2,1)}, bf16[1280,320]{0,1:T(8,128)(2,1)}, bf16[320,1280]{1,0:T(8,128)(2,1)}, ...) | async-done | bytes 9830416 | tf_op jit(solution)/shard_map/psum | solution.py:203
  1574.9 103.7 %reduce-scatter.11.cloned.1.call-done = bf16[1536,1280]{1,0:T(8,128)(2,1)} async-done(((bf16[6144,1280]{1,0:T(8,128)(2,1)}), bf16[1536,1280]{1,0:T(8,128)(2,1)}) %reduce-scatter.11.cloned.1.call-update) | async-done | bytes 3932176 | tf_op jit(solution)/shard_map/reduce_scatter | solution.py:192
  1696.5 40.0 %all-reduce = (f32[1280]{0:T(1024)}, f32[1280]{0:T(1024)}, f32[1280]{0:T(1024)}, f32[3]{0:T(128)S(1)}, f32[]{:T(128)}) all-reduce(f32[1280]{0:T(1024)S(1)} %get-tuple-element.37, f32[1280]{0:T(1024)S(1)} %get-tuple-element.16, f32[1280]{0:T(1024)S(1)} %copy-done.32, ...), channel_id=1, replica_groups=mesh['dp'=8,'mp'=4] {'dp','mp'}, use_global_device_ids=true, to_apply=%region_22.23 | all-reduce | flops 3844 | bytes 30752 | tf_op jit(solution)/shard_map/psum | solution.py:211
  (182 shorter events, 405.7 us)
Async XLA Ops:
  7.2 508.2 %copy-start = (bf16[1280,1280]{1,0:T(8,128)(2,1)S(1)}, bf16[1280,1280]{1,0:T(8,128)(2,1)}, u32[]{:S(2)}) copy-start(bf16[1280,1280]{1,0:T(8,128)(2,1)} %param.20) | copy-start | bytes 9830404
  7.2 112.5 %all-gather.4.cloned.1.call-start = ((), (), s32[]{:S(2)}) async-start(), calls=%async_computation.4 | async-start | bytes 19660800 | tf_op jit(solution)/shard_map/all_gather | solution.py:80
  16.8 389.8 %reduce-scatter.5.cloned.1.call-start = ((), (), s32[]{:S(2)}) async-start(), calls=%async_computation.5 | async-start | bytes 19660800 | tf_op jit(solution)/shard_map/reduce_scatter | solution.py:101
  17.4 121.3 %copy-start.18 = (s32[96,64]{0,1:T(8,128)}, s32[96,64]{0,1:T(8,128)S(1)}, u32[]{:S(2)}) copy-start(s32[96,64]{0,1:T(8,128)S(1)} %convert_reduce_fusion.1) | copy-start | bytes 73732
  286.5 228.9 %all-gather.6.cloned.1.call-start = ((), (), s32[]{:S(2)}) async-start(), calls=%async_computation.6 | async-start | bytes 19660800 | tf_op jit(solution)/shard_map/all_gather | solution.py:109
  287.2 128.0 %copy-start.20 = (f32[1280]{0:T(1024)}, f32[1280]{0:T(1024)S(1)}, u32[]{:S(2)}) copy-start(f32[1280]{0:T(1024)S(1)} %convert_element_type.159) | copy-start | bytes 15364
  415.3 201.5 %all-gather.8.cloned.1.call-start = ((), (), s32[]{:S(2)}) async-start(), calls=%async_computation.8 | async-start | bytes 19660800 | tf_op jit(solution)/shard_map/all_gather | solution.py:133
  415.9 323.3 %reduce-scatter.7.cloned.1.call-start = ((), (), s32[]{:S(2)}) async-start(), calls=%async_computation.7 | async-start | bytes 19660800 | tf_op jit(solution)/shard_map/reduce_scatter | solution.py:115
  515.4 32.7 %copy-start.38 = (bf16[1280,1280]{1,0:T(8,128)(2,1)S(1)}, bf16[1280,1280]{1,0:T(8,128)(2,1)}, u32[]{:S(2)}) copy-start(bf16[1280,1280]{1,0:T(8,128)(2,1)} %param.22) | copy-start | bytes 9830404
  574.1 287.4 %reduce-scatter.9.cloned.1.call-start = ((), (), s32[]{:S(2)}) async-start(), calls=%async_computation.9 | async-start | bytes 19660800 | tf_op jit(solution)/shard_map/reduce_scatter | solution.py:142
  681.2 180.3 %copy-start.21 = (f32[1280]{0:T(1024)S(1)}, f32[1280]{0:T(1024)}, u32[]{:S(2)}) copy-start(f32[1280]{0:T(1024)} %copy-done.20) | copy-start | bytes 15364
  681.2 180.3 %copy-start.24 = (f32[1536]{0:T(1024)S(1)}, f32[1536]{0:T(1024)}, u32[]{:S(2)}) copy-start(f32[1536]{0:T(1024)} %copy-done.23) | copy-start | bytes 18436
  681.3 875.7 %all-reduce.4.cloned.1.call-start = ((), (), s32[]{:S(2)}) async-start(), calls=%async_computation.11 | async-start | bytes 19660800 | tf_op jit(solution)/shard_map/psum | solution.py:203
  861.5 14.0 copy-start.6
  880.9 45.4 %collective-permute-start = (bf16[1536,1280]{1,0:T(8,128)(2,1)}, bf16[1536,1280]{1,0:T(8,128)(2,1)}, u32[]{:S(2)}, u32[]{:S(2)}) collective-permute-start(bf16[1536,1280]{1,0:T(8,128)(2,1)} %fusion.47), channel_id=1, source_target_pairs={{0,1},{1,2},{2,3},{3,0},{4,5},{5,6},{6,7},{7,4},{8,9},{9,10},{10,1... | collective-permute-start | bytes 11796488 | tf_op jit(solution)/shard_map/ppermute | solution.py:21
  926.3 60.1 %collective-permute-start.1 = (bf16[1536,1280]{1,0:T(8,128)(2,1)}, bf16[1536,1280]{1,0:T(8,128)(2,1)S(1)}, u32[]{:S(2)}, u32[]{:S(2)}) collective-permute-start(bf16[1536,1280]{1,0:T(8,128)(2,1)} %collective-permute-done), channel_id=1, source_target_pairs={{0,1},{1,2},{2,3},{3,0},{4,5},{5,6},{6,7},{7,4},{8,9},{9,10},{10,1... | collective-permute-start | bytes 11796488 | tf_op jit(solution)/shard_map/ppermute | solution.py:21
  953.0 58.7 %collective-permute-start.2 = (bf16[1536,1280]{1,0:T(8,128)(2,1)}, bf16[1536,1280]{1,0:T(8,128)(2,1)S(1)}, u32[]{:S(2)}, u32[]{:S(2)}) collective-permute-start(bf16[1536,1280]{1,0:T(8,128)(2,1)} %fusion.47), channel_id=1, source_target_pairs={{0,3},{1,0},{2,1},{3,2},{4,7},{5,4},{6,5},{7,6},{8,11},{9,8},{10,9... | collective-permute-start | bytes 11796488 | tf_op jit(solution)/shard_map/ppermute | solution.py:23
  1242.6 436.0 %reduce-scatter.11.cloned.1.call-start = ((), (), s32[]{:S(2)}) async-start(), calls=%async_computation.10 | async-start | bytes 19660800 | tf_op jit(solution)/shard_map/reduce_scatter | solution.py:192
  1565.8 112.8 %copy-start.27 = (f32[1280]{0:T(1024)S(1)}, f32[1280]{0:T(1024)}, u32[]{:S(2)}) copy-start(f32[1280]{0:T(1024)} %copy-done.26) | copy-start | bytes 15364
  1565.8 112.8 %copy-start.29 = (f32[1536]{0:T(1024)S(1)}, f32[1536]{0:T(1024)}, u32[]{:S(2)}) copy-start(f32[1536]{0:T(1024)} %copy-done.28) | copy-start | bytes 18436
  1570.3 113.8 %copy-start.22 = (f32[1280]{0:T(1024)S(1)}, f32[1280]{0:T(1024)}, u32[]{:S(2)}) copy-start(f32[1280]{0:T(1024)} %copy-done.20) | copy-start | bytes 15364
  1570.3 113.8 %copy-start.25 = (f32[1536]{0:T(1024)S(1)}, f32[1536]{0:T(1024)}, u32[]{:S(2)}) copy-start(f32[1536]{0:T(1024)} %copy-done.23) | copy-start | bytes 18436
  1570.3 113.8 %copy-start.31 = (f32[1536]{0:T(1024)S(1)}, f32[1536]{0:T(1024)}, u32[]{:S(2)}) copy-start(f32[1536]{0:T(1024)} %copy-done.30) | copy-start | bytes 18436
  1684.1 53.6 %copy-start.1 = (bf16[1280,1280]{1,0:T(8,128)(2,1)S(1)}, bf16[1280,1280]{1,0:T(8,128)(2,1)}, u32[]{:S(2)}) copy-start(bf16[1280,1280]{1,0:T(8,128)(2,1)} %param.20) | copy-start | bytes 9830404
  (31 other events, 206.9 us)
Sparse Core Ops, SparseCore 0:
  16.9 102.6 all-gather.3
  286.7 119.8 reduce-scatter.4
  415.4 99.9 all-gather.5
  516.8 99.9 all-gather.7
  619.3 119.8 reduce-scatter.6
  741.6 119.8 reduce-scatter.8
  1242.7 314.1 all-reduce.3
  1559.7 118.8 reduce-scatter.10
